TPU v7x, 256 devices: a whole 4x4x8 slice. The times are simulated.
256 devices in a mesh: inst: 32 (over z_lo, y, x), tp: 8 (over z_hi, core).
Axes of the slice: x: 4, y: 4, z: 8 (z_hi: 4, z_lo: 2; z = z_hi * 2 + z_lo), core: 2. Of those that a mesh axis runs over, the one named last changes fastest.
Arguments:
- kv_cache: bfloat16 [256, 2048, 2048], P('inst', None, 'tp'), may hold values from -8 to 8
- queries: bfloat16 [384, 6, 8192], P('inst', None, 'tp'), may hold values from -8 to 8
- fresh_kv: bfloat16 [384, 6, 2048], P('inst', None, 'tp'), may hold values from -6 to 6
- out_proj: bfloat16 [8192, 4096], P('tp'), may hold values from -0.0625 to 0.0625
- moving: int32 [128], replicated, may hold values from 0 to 255, as said below
- destination: int32 [128], replicated, may hold values from 0 to 31, as said below
- round_pages: int32 [128, 3], replicated, may hold values from 0 to 8, as said below
- lengths: int32 [256], replicated, may hold values from 1 to 2042, as said below
Outputs:
- attended: bfloat16 [384, 6, 4096], P('inst', None, 'tp')
- arrived_cache: bfloat16 [128, 2048, 2048], P('inst', None, 'tp')
Inputs may be any that keep to these rules, and one draw needn't show every extreme that they name: `moving`: each instance sends 4 distinct rows of its own. (destination[m] - moving[m] // 8) mod 32 is 1, 2, 8 or 16; every instance sends one row at each of these distances and receives one from each. round_pages[m, 0] >= 1, and a row's counts sum to ceil(lengths[moving[m]] / 128); some row sends 8 pages in one round. `lengths`: migrating rows are longer than 1792; some migrating row has the largest length.
All inputs are finite; a program needn't handle non-finite values.
Results may differ from a plain program's by a relative error of at most 0.0057.
Values may be sent and summed in bfloat16 or wider, within the bound.
A program may use at most 128 MiB of HBM per device.

v0:
```python
import jax
import jax.numpy as jnp
from jax import lax
from jax.sharding import PartitionSpec as P

HEAD_DIM = 128
PAGE = 128
R_DEV = 8
PG_CAP = 8


minus_large = -1e30


def passed_along(value, axis, steps):
    count = lax.axis_size(axis)
    pairs = [(source, (source + steps) % count) for source in range(count)]
    return lax.ppermute(value, axis, pairs)


def plan_tables(moving, destination, round_pages, lengths, inst_count):
    source_inst = moving // R_DEV
    distance = (destination - source_inst) % inst_count
    distances = jnp.array([1, 2, inst_count // 4, inst_count // 2], jnp.int32)
    lane_index = jnp.sum(
        jnp.where(
            distance[:, None] == distances[None, :], jnp.arange(4, dtype=jnp.int32)[None, :], 0
        ),
        axis=1,
    )
    done_round = jnp.max(
        jnp.where(round_pages > 0, jnp.arange(round_pages.shape[1], dtype=jnp.int32)[None, :], 0),
        axis=1,
    )
    base_length = jnp.take(lengths, moving)
    return (source_inst, lane_index, done_round, base_length)


def attend(stored, length, query_rows, fresh_rows, active, first_step):
    slot_total, key_count, row_width = stored.shape
    kv_local = row_width // (2 * HEAD_DIM)
    step_count = query_rows.shape[1]
    fresh_count = fresh_rows.shape[1]
    group_size = query_rows.shape[2] // (kv_local * HEAD_DIM)
    keys_all = stored.reshape(slot_total, key_count, kv_local, 2, HEAD_DIM)
    fresh_all = fresh_rows.reshape(slot_total, fresh_count, kv_local, 2, HEAD_DIM)
    query_heads = query_rows.reshape(slot_total, step_count, kv_local, group_size, HEAD_DIM)
    score_scale = HEAD_DIM ** (-0.5)
    cache_scores = (
        jnp.einsum(
            "stkgd,slkd->stkgl",
            query_heads,
            keys_all[:, :, :, 0],
            preferred_element_type=jnp.float32,
        )
        * score_scale
    )
    fresh_scores = (
        jnp.einsum(
            "stkgd,sukd->stkgu",
            query_heads,
            fresh_all[:, :, :, 0],
            preferred_element_type=jnp.float32,
        )
        * score_scale
    )
    cache_ok = jnp.arange(key_count)[None, :] < length[:, None]
    step_ids = jnp.arange(fresh_count)
    fresh_ok = (
        step_ids[None, None, :] <= (first_step + jnp.arange(step_count))[None, :, None]
    ) & active[:, None, :]
    cache_scores = jnp.where(cache_ok[:, None, None, None, :], cache_scores, minus_large)
    fresh_scores = jnp.where(fresh_ok[:, :, None, None, :], fresh_scores, minus_large)
    top_score = jnp.maximum(jnp.max(cache_scores, axis=-1), jnp.max(fresh_scores, axis=-1))
    cache_exp = jnp.exp(cache_scores - top_score[..., None])
    fresh_exp = jnp.exp(fresh_scores - top_score[..., None])
    denominator = jnp.sum(cache_exp, axis=-1) + jnp.sum(fresh_exp, axis=-1)
    cache_weight = (cache_exp / denominator[..., None]).astype(jnp.bfloat16)
    fresh_weight = (fresh_exp / denominator[..., None]).astype(jnp.bfloat16)
    mixed_values = jnp.einsum(
        "stkgl,slkd->stkgd", cache_weight, keys_all[:, :, :, 1], preferred_element_type=jnp.float32
    )
    mixed_values = mixed_values + jnp.einsum(
        "stkgu,sukd->stkgd", fresh_weight, fresh_all[:, :, :, 1], preferred_element_type=jnp.float32
    )
    return mixed_values.reshape(slot_total, step_count, kv_local * group_size * HEAD_DIM).astype(
        jnp.bfloat16
    )


def local(kv_cache, queries, fresh_kv, out_proj, moving, destination, round_pages, lengths):
    inst_count = lax.axis_size("inst")
    inst_index = lax.axis_index("inst")
    cache_len = kv_cache.shape[1]
    row_width = kv_cache.shape[2]
    step_total = queries.shape[1]
    round_total = round_pages.shape[1]
    round_size = step_total // round_total
    lane_total = queries.shape[0] - R_DEV
    distances = [1, 2, inst_count // 4, inst_count // 2]
    source_inst, lane_index, done_round, base_length = plan_tables(
        moving, destination, round_pages, lengths, inst_count
    )
    lane_ids = jnp.arange(lane_total)
    own_match = (source_inst == inst_index)[None, :] & (lane_index[None, :] == lane_ids[:, None])
    sending = jnp.any(own_match, axis=1)
    own_rows = jnp.sum(jnp.where(own_match, moving[None, :] - inst_index * R_DEV, 0), axis=1)
    own_length = jnp.sum(jnp.where(own_match, base_length[None, :], 0), axis=1)
    own_pages = jnp.sum(jnp.where(own_match[:, :, None], round_pages[None, :, :], 0), axis=1)
    zero_value = jnp.zeros((), kv_cache.dtype)
    positions = jnp.arange(cache_len)
    own_blocks = jnp.take(kv_cache, own_rows, axis=0)
    own_blocks = jnp.where(
        ((positions[None, :] < own_length[:, None]) & sending[:, None])[:, :, None],
        own_blocks,
        zero_value,
    )
    matched = (destination[None, :] == inst_index) & (lane_index[None, :] == lane_ids[:, None])
    arriving = jnp.any(matched, axis=1)
    arrival_length = jnp.sum(jnp.where(matched, base_length[None, :], 0), axis=1)
    arrival_done = jnp.sum(jnp.where(matched, done_round[None, :], 0), axis=1)
    arrival_pages = jnp.sum(jnp.where(matched[:, :, None], round_pages[None, :, :], 0), axis=1)
    home_rows = inst_index * R_DEV + jnp.arange(R_DEV)
    staying = jnp.logical_not(jnp.any(moving[None, :] == home_rows[:, None], axis=1))
    home_length = lax.dynamic_slice_in_dim(lengths, inst_index * R_DEV, R_DEV)
    step_ids = jnp.arange(step_total)
    home_active = staying[:, None] & (step_ids[None, :] >= 0)
    arrival_active = arriving[:, None] & ((step_ids // round_size)[None, :] > arrival_done[:, None])
    span_rows = PG_CAP * PAGE
    padded = jnp.concatenate(
        [own_blocks, jnp.zeros((lane_total, span_rows, row_width), kv_cache.dtype)], axis=1
    )
    landed = jnp.zeros((lane_total, cache_len + span_rows, row_width), kv_cache.dtype)
    outputs_list = []
    for round_number in range(round_total):
        sent_before = jnp.sum(own_pages[:, :round_number], axis=1)
        received_before = jnp.sum(arrival_pages[:, :round_number], axis=1)
        for lane_number in range(lane_total):
            page_block = lax.dynamic_slice_in_dim(
                padded[lane_number], sent_before[lane_number] * PAGE, span_rows, 0
            )
            page_block = jnp.where(
                (jnp.arange(span_rows) < own_pages[lane_number, round_number] * PAGE)[:, None],
                page_block,
                zero_value,
            )
            incoming = passed_along(page_block, "inst", distances[lane_number])
            lane_block = lax.dynamic_update_slice_in_dim(
                landed[lane_number], incoming, received_before[lane_number] * PAGE, 0
            )
            landed = landed.at[lane_number].set(lane_block)
        first_step = round_number * round_size
        step_range = slice(first_step, first_step + round_size)
        home_out = attend(
            kv_cache,
            home_length,
            queries[:R_DEV, step_range],
            fresh_kv[:R_DEV],
            home_active,
            first_step,
        )
        arrival_out = attend(
            landed,
            arrival_length,
            queries[R_DEV:, step_range],
            fresh_kv[R_DEV:],
            arrival_active,
            first_step,
        )
        heads_out = jnp.concatenate([home_out, arrival_out], axis=0)
        round_active = jnp.concatenate([home_active, arrival_active], axis=0)[:, step_range]
        slot_total = heads_out.shape[0]
        projected = jnp.dot(
            heads_out.reshape(slot_total * round_size, -1),
            out_proj,
            preferred_element_type=jnp.float32,
        )
        projected = projected.reshape(slot_total, round_size, -1)
        projected = jnp.where(round_active[:, :, None], projected, 0.0)
        outputs_list.append(
            lax.psum_scatter(projected, "tp", scatter_dimension=2, tiled=True).astype(jnp.bfloat16)
        )
    attended = jnp.concatenate(outputs_list, axis=1)
    result_cache = landed[:, :cache_len]
    decoded_first = round_size * (arrival_done + 1)
    offset_rows = jnp.arange(step_total)
    for lane_number in range(lane_total):
        picked = jnp.take(
            fresh_kv[R_DEV + lane_number],
            jnp.minimum(decoded_first[lane_number] + offset_rows, step_total - 1),
            axis=0,
        )
        usable_rows = arriving[lane_number] & (
            decoded_first[lane_number] + offset_rows < step_total
        )
        window = lax.dynamic_slice_in_dim(
            result_cache[lane_number], arrival_length[lane_number], step_total, 0
        )
        window = jnp.where(usable_rows[:, None], picked, window)
        updated = lax.dynamic_update_slice_in_dim(
            result_cache[lane_number], window, arrival_length[lane_number], 0
        )
        result_cache = result_cache.at[lane_number].set(updated)
    return (attended, result_cache)


def solution(mesh):
    in_specs = (
        P("inst", None, "tp"),
        P("inst", None, "tp"),
        P("inst", None, "tp"),
        P("tp", None),
        P(),
        P(),
        P(),
        P(),
    )
    out_specs = (P("inst", None, "tp"), P("inst", None, "tp"))
    return jax.shard_map(local, mesh=mesh, in_specs=in_specs, out_specs=out_specs, check_vma=False)
```

profile of v0, /device:TPU:1, one launch (start us, length us, event | category | flops | bytes accessed | tf_op | source)
XLA Modules:
  0.0 402.5 jit_solution(13539744040842451947)
XLA Ops:
  11.3 1.6 gather_fusion
  18.3 6.2 %gather_fusion.1 = bf16[4,2048,256]{2,1,0:T(8,128)(2,1)} fusion(bf16[8,2048,256]{2,1,0:T(8,128)(2,1)} %param.43, s32[1024]{0:T(1024)S(1)} %pad_clamp_fusion.4), kind=kCustom, calls=%fused_computation.5 | custom fusion | bytes 8388624 | tf_op jit(solution)/shard_map/jit(_take)/gather | solution.py:112
  24.5 3.6 select_select_fusion
  28.1 2.0 copy-done.2
  30.2 2.4 fusion.81
  32.6 2.5 collective-permute-start.3
  35.0 2.9 collective-permute-start.2
  38.0 2.7 collective-permute-start.1
  42.3 3.8 pad_slice_fusion
  47.4 2.6 bitcast_select_fusion
  52.9 1.7 compare_and_fusion
  54.6 1.8 compare_select_fusion
  59.8 11.6 %copy.158 = bf16[8,2048,256]{1,2,0:T(8,128)(2,1)} copy(bf16[8,2048,256]{2,1,0:T(8,128)(2,1)} %param.43) | data formatting | bytes 16777216 | tf_op args[0]
  74.0 1.9 compare_and_fusion.2
  75.9 1.3 compare_select_fusion.2
  87.5 3.1 fusion.169
  90.6 3.5 fusion.165
  96.3 1.2 fusion.61
  98.1 1.2 fusion.62
  100.0 1.2 fusion.60
  101.9 2.6 bitcast_select_fusion.2
  104.5 1.6 bitcast_select_fusion.1
  107.8 1.5 bitcast_select_fusion.3
  126.4 1.3 compare_and_fusion.3
  127.7 1.5 collective-permute-start.7
  131.4 1.8 collective-permute-start.9
  134.6 1.5 collective-permute-start.5
  138.7 2.6 copy-done
  141.4 8.7 %copy.168 = bf16[4,3072,256]{1,2,0:T(8,128)(2,1)} copy(bf16[4,3072,256]{2,1,0:T(8,128)(2,1)} %copy-done) | data formatting | bytes 12582912 | tf_op jit(solution)/shard_map/scatter | solution.py:151
  150.2 28.4 %collective-permute-done.4 = bf16[1024,256]{1,0:T(8,128)(2,1)} collective-permute-done((bf16[1024,256]{1,0:T(8,128)(2,1)}, bf16[1024,256]{1,0:T(8,128)(2,1)}, u32[]{:S(2)}, u32[]{:S(2)}) %collective-permute-start.4) | collective-permute-done | bytes 524320 | tf_op jit(solution)/shard_map/ppermute | solution.py:18
  179.6 1.3 constant_dynamic-update-slice_fusion.11
  180.9 1.5 slice.750
  182.4 2.9 collective-permute-start.6
  187.7 1.5 slice.751
  189.2 11.4 %collective-permute-done.6 = bf16[1024,256]{1,0:T(8,128)(2,1)S(1)} collective-permute-done((bf16[1024,256]{1,0:T(8,128)(2,1)S(1)}, bf16[1024,256]{1,0:T(8,128)(2,1)S(1)}, u32[]{:S(2)}, u32[]{:S(2)}) %collective-permute-start.6) | collective-permute-done | bytes 524320 | tf_op jit(solution)/shard_map/ppermute | solution.py:18
  200.7 1.3 constant_dynamic-update-slice_fusion.9
  202.0 1.5 slice.752
  204.6 1.3 constant_dynamic-update-slice_fusion.8
  205.9 1.5 slice.755
  207.4 8.6 %copy.181 = bf16[4,3072,256]{1,2,0:T(8,128)(2,1)} copy(bf16[4,3072,256]{2,1,0:T(8,128)(2,1)} %constant_dynamic-update-slice_fusion.8) | data formatting | bytes 12582912 | tf_op jit(solution)/shard_map/scatter | solution.py:151
  217.1 1.3 constant_dynamic-update-slice_fusion.7
  218.4 1.5 slice.756
  222.3 1.5 slice.757
  224.9 1.3 constant_dynamic-update-slice_fusion.5
  226.1 1.5 slice.758
  228.7 1.3 constant_dynamic-update-slice_fusion.4
  230.0 1.3 slice.762
  231.3 4.5 %slice.761 = bf16[4,2048,256]{2,1,0:T(8,128)(2,1)} slice(bf16[4,3072,256]{2,1,0:T(8,128)(2,1)} %constant_dynamic-update-slice_fusion.4), slice={[0:4], [0:2048], [0:256]} | slice | bytes 8388608 | tf_op jit(solution)/shard_map/slice | solution.py:184
  235.8 8.7 %copy.191 = bf16[4,3072,256]{1,2,0:T(8,128)(2,1)} copy(bf16[4,3072,256]{2,1,0:T(8,128)(2,1)} %constant_dynamic-update-slice_fusion.4) | data formatting | bytes 12582912 | tf_op jit(solution)/shard_map/scatter | solution.py:151
  244.5 2.5 fusion.171
  247.3 2.5 fusion.167
  250.5 2.9 fusion.73
  253.6 2.5 fusion.163
  256.7 2.9 fusion.74
  260.6 1.3 slice.763
  261.9 5.7 %fusion.9 = f32[12,2,4096]{2,0,1:T(8,128)} fusion(bf16[1024,4096]{1,0:T(8,128)(2,1)} %param.46, pred[12,2]{0,1:T(4,128)(4,1)S(1)} %copy-done.13, bf16[4,2,1024]{2,0,1:T(4,128)(2,1)S(1)} %copy.186, bf16[8,2,1024]{2,0,1:T(8,128)(2,1)S(1)} %copy.185), kind=kOutput, calls=%fused_computation.17 | convolution fusion | flops 201523200 | bytes 8831000 | tf_op jit(solution)/shard_map/dot_general | solution.py:173
  267.8 2.9 fusion.72
  270.7 5.7 %fusion.12 = f32[12,2,4096]{2,0,1:T(8,128)} fusion(bf16[1024,4096]{1,0:T(8,128)(2,1)} %param.46, pred[12,2]{0,1:T(4,128)(4,1)S(1)} %copy-done.12, bf16[4,2,1024]{2,0,1:T(4,128)(2,1)S(1)} %copy.196, bf16[8,2,1024]{2,0,1:T(8,128)(2,1)S(1)} %copy.195), kind=kOutput, calls=%fused_computation.18 | convolution fusion | flops 201523200 | bytes 8831000 | tf_op jit(solution)/shard_map/dot_general | solution.py:173
  277.8 1.3 slice.764
  279.1 5.7 %fusion.6 = f32[12,2,4096]{2,0,1:T(8,128)} fusion(bf16[1024,4096]{1,0:T(8,128)(2,1)} %param.46, pred[12,2]{0,1:T(4,128)(4,1)S(1)} %copy-done.11, bf16[4,2,1024]{2,0,1:T(4,128)(2,1)S(1)} %copy.176, bf16[8,2,1024]{2,0,1:T(8,128)(2,1)S(1)} %copy.175), kind=kOutput, calls=%fused_computation.16 | convolution fusion | flops 201523200 | bytes 8831000 | tf_op jit(solution)/shard_map/dot_general | solution.py:173
  286.1 1.3 slice.765
  288.6 29.3 %reduce-scatter.6.cloned.1.call-done = f32[12,2,512]{2,0,1:T(8,128)} async-done(((f32[12,2,4096]{2,0,1:T(8,128)}), f32[12,2,512]{2,0,1:T(8,128)}) %reduce-scatter.6.cloned.1.call-update) | async-done | bytes 49168 | tf_op jit(solution)/shard_map/reduce_scatter | solution.py:181
  318.8 37.5 %reduce-scatter.8.cloned.1.call-done = f32[12,2,512]{2,0,1:T(8,128)} async-done(((f32[12,2,4096]{2,0,1:T(8,128)}), f32[12,2,512]{2,0,1:T(8,128)}) %reduce-scatter.8.cloned.1.call-update) | async-done | bytes 49168 | tf_op jit(solution)/shard_map/reduce_scatter | solution.py:181
  357.1 37.3 %reduce-scatter.4.cloned.1.call-done = f32[12,2,512]{2,0,1:T(8,128)} async-done(((f32[12,2,4096]{2,0,1:T(8,128)}), f32[12,2,512]{2,0,1:T(8,128)}) %reduce-scatter.4.cloned.1.call-update) | async-done | bytes 49168 | tf_op jit(solution)/shard_map/reduce_scatter | solution.py:181
  (253 shorter events, 56.8 us)
Async XLA Ops:
  7.2 310.8 %reduce-scatter.6.cloned.1.call-start = ((), (), s32[]{:S(2)}) async-start(), calls=%async_computation.4 | async-start | bytes 589824 | tf_op jit(solution)/shard_map/reduce_scatter | solution.py:181
  13.9 38.3 %copy-start.19 = (s32[4]{0:T(128)}, s32[4]{0:T(128)S(1)}, u32[]{:S(2)}) copy-start(s32[4]{0:T(128)S(1)} %get-tuple-element.210) | copy-start | bytes 52
  28.1 2.0 copy-start.2
  32.6 104.8 %collective-permute-start.3 = (bf16[1024,256]{1,0:T(8,128)(2,1)}, bf16[1024,256]{1,0:T(8,128)(2,1)}, u32[]{:S(2)}, u32[]{:S(2)}) collective-permute-start(bf16[1024,256]{1,0:T(8,128)(2,1)} %get-tuple-element.221), channel_id=1, source_target_pairs={{0,128},{8,136},{16,144},{24,152},{32,160},{40,168},{48,176},{56,1... | collective-permute-start | bytes 1572872 | tf_op jit(solution)/shard_map/ppermute | solution.py:18
  35.0 99.5 %collective-permute-start.2 = (bf16[1024,256]{1,0:T(8,128)(2,1)}, bf16[1024,256]{1,0:T(8,128)(2,1)}, u32[]{:S(2)}, u32[]{:S(2)}) collective-permute-start(bf16[1024,256]{1,0:T(8,128)(2,1)} %get-tuple-element.222), channel_id=1, source_target_pairs={{0,64},{8,72},{16,80},{24,88},{32,96},{40,104},{48,112},{56,120},{... | collective-permute-start | bytes 1572872 | tf_op jit(solution)/shard_map/ppermute | solution.py:18
  38.0 92.9 %collective-permute-start.1 = (bf16[1024,256]{1,0:T(8,128)(2,1)}, bf16[1024,256]{1,0:T(8,128)(2,1)}, u32[]{:S(2)}, u32[]{:S(2)}) collective-permute-start(bf16[1024,256]{1,0:T(8,128)(2,1)} %get-tuple-element.223), channel_id=1, source_target_pairs={{0,16},{8,24},{16,32},{24,40},{32,48},{40,56},{48,64},{56,72},{64,... | collective-permute-start | bytes 1572872 | tf_op jit(solution)/shard_map/ppermute | solution.py:18
  40.7 87.0 %collective-permute-start = (bf16[1024,256]{1,0:T(8,128)(2,1)}, bf16[1024,256]{1,0:T(8,128)(2,1)}, u32[]{:S(2)}, u32[]{:S(2)}) collective-permute-start(bf16[1024,256]{1,0:T(8,128)(2,1)} %get-tuple-element.224), channel_id=1, source_target_pairs={{0,8},{8,16},{16,24},{24,32},{32,40},{40,48},{48,56},{56,64},{64,7... | collective-permute-start | bytes 1572872 | tf_op jit(solution)/shard_map/ppermute | solution.py:18
  42.3 16.7 %copy-start.7 = (bf16[12,6,256]{2,1,0:T(8,128)(2,1)S(1)}, bf16[12,6,256]{2,1,0:T(8,128)(2,1)}, u32[]{:S(2)}) copy-start(bf16[12,6,256]{2,1,0:T(8,128)(2,1)} %param.45) | copy-start | bytes 110596
  42.3 16.7 %copy-start.8 = (bf16[12,6,1024]{2,1,0:T(8,128)(2,1)S(1)}, bf16[12,6,1024]{2,1,0:T(8,128)(2,1)}, u32[]{:S(2)}) copy-start(bf16[12,6,1024]{2,1,0:T(8,128)(2,1)} %param.44) | copy-start | bytes 442372
  50.0 177.6 %collective-permute-start.11 = (bf16[1024,256]{1,0:T(8,128)(2,1)}, bf16[1024,256]{1,0:T(8,128)(2,1)}, u32[]{:S(2)}, u32[]{:S(2)}) collective-permute-start(bf16[1024,256]{1,0:T(8,128)(2,1)} %get-tuple-element.225), channel_id=1, source_target_pairs={{0,128},{8,136},{16,144},{24,152},{32,160},{40,168},{48,176},{56,1... | collective-permute-start | bytes 1572872 | tf_op jit(solution)/shard_map/ppermute | solution.py:18
  59.7 11.7 %copy-start.1 = (s32[256]{0:T(256)S(1)}, s32[256]{0:T(256)}, u32[]{:S(2)}) copy-start(s32[256]{0:T(256)} %param.50) | copy-start | bytes 3076
  59.7 11.8 %copy-start.18 = (s32[128]{0:T(128)S(1)}, s32[128]{0:T(128)}, u32[]{:S(2)}) copy-start(s32[128]{0:T(128)} %param.47) | copy-start | bytes 1540
  59.7 11.8 %copy-start.33 = (s32[8]{0:T(128)S(1)}, s32[8]{0:T(128)}, u32[]{:S(2)}) copy-start(s32[8]{0:T(128)} %iota_add_fusion.6) | copy-start | bytes 100
  59.7 12.6 %copy-start.20 = (s32[4]{0:T(128)S(1)}, s32[4]{0:T(128)}, u32[]{:S(2)}) copy-start(s32[4]{0:T(128)} %copy-done.19) | copy-start | bytes 52
  59.7 12.6 %copy-start.32 = (s32[6]{0:T(128)S(1)}, s32[6]{0:T(128)}, u32[]{:S(2)}) copy-start(s32[6]{0:T(128)} %and_select_fusion.1) | copy-start | bytes 76
  59.8 12.8 %copy-start.30 = (s32[2]{0:T(128)S(1)}, s32[2]{0:T(128)}, u32[]{:S(2)}) copy-start(s32[2]{0:T(128)} %iota_add_fusion.5) | copy-start | bytes 28
  59.8 12.8 %copy-start.31 = (s32[2]{0:T(128)S(1)}, s32[2]{0:T(128)}, u32[]{:S(2)}) copy-start(s32[2]{0:T(128)} %iota_add_fusion.4) | copy-start | bytes 28
  59.8 18.1 %copy-start.22 = (s32[6]{0:T(128)S(1)}, s32[6]{0:T(128)}, u32[]{:S(2)}) copy-start(s32[6]{0:T(128)} %get-tuple-element.320) | copy-start | bytes 76
  59.8 18.7 %copy-start.21 = (s32[6]{0:T(128)S(1)}, s32[6]{0:T(128)}, u32[]{:S(2)}) copy-start(s32[6]{0:T(128)} %get-tuple-element.321) | copy-start | bytes 76
  59.8 27.4 %slice-start = ((bf16[12,6,256]{2,1,0:T(8,128)(2,1)}), bf16[4,6,256]{2,1,0:T(8,128)(2,1)S(1)}, s32[]{:S(2)}) async-start(bf16[12,6,256]{2,1,0:T(8,128)(2,1)} %param.45), calls=%async_computation.6 | async-start | bytes 32768 | tf_op jit(solution)/shard_map/slice | solution.py:166
  59.8 27.4 %slice-start.1 = ((bf16[12,6,256]{2,1,0:T(8,128)(2,1)}), bf16[8,6,256]{2,1,0:T(8,128)(2,1)S(1)}, s32[]{:S(2)}) async-start(bf16[12,6,256]{2,1,0:T(8,128)(2,1)} %param.45), calls=%async_computation.7 | async-start | bytes 65536 | tf_op jit(solution)/shard_map/slice | solution.py:158
  59.8 27.5 %copy-start.9 = (bf16[4,2,1024]{2,1,0:T(2,128)(2,1)S(1)}, bf16[4,2,1024]{2,1,0:T(2,128)(2,1)}, u32[]{:S(2)}) copy-start(bf16[4,2,1024]{2,1,0:T(2,128)(2,1)} %get-tuple-element.236) | copy-start | bytes 49156
  87.5 7.2 %copy-start.3 = (bf16[8,2048,256]{1,2,0:T(8,128)(2,1)S(1)}, bf16[8,2048,256]{1,2,0:T(8,128)(2,1)}, u32[]{:S(2)}) copy-start(bf16[8,2048,256]{1,2,0:T(8,128)(2,1)} %copy.158) | copy-start | bytes 25165828
  99.9 1.7 copy-start.23
  99.9 2.0 copy-start.28
  100.0 2.0 copy-start.29
  100.0 4.5 %copy-start.26 = (pred[1024]{0:T(1024)(128)(4,1)S(1)}, pred[1024]{0:T(1024)(128)(4,1)}, u32[]{:S(2)}) copy-start(pred[1024]{0:T(1024)(128)(4,1)} %iota_compare_fusion.4) | copy-start | bytes 3076
  100.0 4.5 %copy-start.27 = (pred[1024]{0:T(1024)(128)(4,1)S(1)}, pred[1024]{0:T(1024)(128)(4,1)}, u32[]{:S(2)}) copy-start(pred[1024]{0:T(1024)(128)(4,1)} %iota_compare_fusion.8) | copy-start | bytes 3076
  101.2 6.6 %copy-start.24 = (pred[1024]{0:T(1024)(128)(4,1)S(1)}, pred[1024]{0:T(1024)(128)(4,1)}, u32[]{:S(2)}) copy-start(pred[1024]{0:T(1024)(128)(4,1)} %iota_compare_fusion.6) | copy-start | bytes 3076
  101.2 6.6 %copy-start.25 = (pred[1024]{0:T(1024)(128)(4,1)S(1)}, pred[1024]{0:T(1024)(128)(4,1)}, u32[]{:S(2)}) copy-start(pred[1024]{0:T(1024)(128)(4,1)} %iota_compare_fusion.10) | copy-start | bytes 3076
  127.7 75.8 %collective-permute-start.7 = (bf16[1024,256]{1,0:T(8,128)(2,1)}, bf16[1024,256]{1,0:T(8,128)(2,1)}, u32[]{:S(2)}, u32[]{:S(2)}) collective-permute-start(bf16[1024,256]{1,0:T(8,128)(2,1)} %get-tuple-element.226), channel_id=1, source_target_pairs={{0,128},{8,136},{16,144},{24,152},{32,160},{40,168},{48,176},{56,1... | collective-permute-start | bytes 1572872 | tf_op jit(solution)/shard_map/ppermute | solution.py:18
  130.4 1.0 copy-start.5
  131.4 88.5 %collective-permute-start.9 = (bf16[1024,256]{1,0:T(8,128)(2,1)S(1)}, bf16[1024,256]{1,0:T(8,128)(2,1)}, u32[]{:S(2)}, u32[]{:S(2)}) collective-permute-start(bf16[1024,256]{1,0:T(8,128)(2,1)S(1)} %copy-done.5), channel_id=1, source_target_pairs={{0,16},{8,24},{16,32},{24,40},{32,48},{40,56},{48,64},{56,72},{64,... | collective-permute-start | bytes 1572872 | tf_op jit(solution)/shard_map/ppermute | solution.py:18
  134.6 47.9 %collective-permute-start.5 = (bf16[1024,256]{1,0:T(8,128)(2,1)}, bf16[1024,256]{1,0:T(8,128)(2,1)}, u32[]{:S(2)}, u32[]{:S(2)}) collective-permute-start(bf16[1024,256]{1,0:T(8,128)(2,1)} %get-tuple-element.230), channel_id=1, source_target_pairs={{0,16},{8,24},{16,32},{24,40},{32,48},{40,56},{48,64},{56,72},{64,... | collective-permute-start | bytes 1572872 | tf_op jit(solution)/shard_map/ppermute | solution.py:18
  137.4 41.1 %collective-permute-start.4 = (bf16[1024,256]{1,0:T(8,128)(2,1)}, bf16[1024,256]{1,0:T(8,128)(2,1)}, u32[]{:S(2)}, u32[]{:S(2)}) collective-permute-start(bf16[1024,256]{1,0:T(8,128)(2,1)} %get-tuple-element.232), channel_id=1, source_target_pairs={{0,8},{8,16},{16,24},{24,32},{32,40},{40,48},{48,56},{56,64},{64,7... | collective-permute-start | bytes 1572872 | tf_op jit(solution)/shard_map/ppermute | solution.py:18
  138.7 2.6 copy-start
  141.4 37.1 %copy-start.4 = (bf16[1024,256]{1,0:T(8,128)(2,1)S(1)}, bf16[1024,256]{1,0:T(8,128)(2,1)}, u32[]{:S(2)}) copy-start(bf16[1024,256]{1,0:T(8,128)(2,1)} %get-tuple-element.227) | copy-start | bytes 1572868
  150.2 32.3 %copy-start.6 = (bf16[1024,256]{1,0:T(8,128)(2,1)S(1)}, bf16[1024,256]{1,0:T(8,128)(2,1)}, u32[]{:S(2)}) copy-start(bf16[1024,256]{1,0:T(8,128)(2,1)} %get-tuple-element.228) | copy-start | bytes 1572868
  178.5 45.2 %collective-permute-start.10 = (bf16[1024,256]{1,0:T(8,128)(2,1)S(1)}, bf16[1024,256]{1,0:T(8,128)(2,1)}, u32[]{:S(2)}, u32[]{:S(2)}) collective-permute-start(bf16[1024,256]{1,0:T(8,128)(2,1)S(1)} %copy-done.4), channel_id=1, source_target_pairs={{0,64},{8,72},{16,80},{24,88},{32,96},{40,104},{48,112},{56,120},{... | collective-permute-start | bytes 1572872 | tf_op jit(solution)/shard_map/ppermute | solution.py:18
  182.4 18.2 %collective-permute-start.6 = (bf16[1024,256]{1,0:T(8,128)(2,1)S(1)}, bf16[1024,256]{1,0:T(8,128)(2,1)S(1)}, u32[]{:S(2)}, u32[]{:S(2)}) collective-permute-start(bf16[1024,256]{1,0:T(8,128)(2,1)S(1)} %copy-done.6), channel_id=1, source_target_pairs={{0,64},{8,72},{16,80},{24,88},{32,96},{40,104},{48,112},{56,120},{... | collective-permute-start | bytes 1572872 | tf_op jit(solution)/shard_map/ppermute | solution.py:18
  200.7 15.4 %collective-permute-start.8 = (bf16[1024,256]{1,0:T(8,128)(2,1)S(1)}, bf16[1024,256]{1,0:T(8,128)(2,1)}, u32[]{:S(2)}, u32[]{:S(2)}) collective-permute-start(bf16[1024,256]{1,0:T(8,128)(2,1)S(1)} %get-tuple-element.231), channel_id=1, source_target_pairs={{0,8},{8,16},{16,24},{24,32},{32,40},{40,48},{48,56},{56,64},{64,7... | collective-permute-start | bytes 1572872 | tf_op jit(solution)/shard_map/ppermute | solution.py:18
  235.8 8.7 %copy-start.10 = (pred[4,3072]{1,0:T(4,128)(4,1)S(1)}, pred[4,3072]{1,0:T(4,128)(4,1)}, u32[]{:S(2)}) copy-start(pred[4,3072]{1,0:T(4,128)(4,1)} %iota_compare_fusion.1) | copy-start | bytes 36868
  256.7 5.3 %copy-start.13 = (pred[12,2]{0,1:T(4,128)(4,1)S(1)}, pred[12,2]{0,1:T(4,128)(4,1)}, u32[]{:S(2)}) copy-start(pred[12,2]{0,1:T(4,128)(4,1)} %get-tuple-element.265) | copy-start | bytes 76
  267.7 2.9 copy-start.12
  267.7 88.5 %reduce-scatter.8.cloned.1.call-start = ((), (), s32[]{:S(2)}) async-start(), calls=%async_computation.5 | async-start | bytes 589824 | tf_op jit(solution)/shard_map/reduce_scatter | solution.py:181
  270.6 5.8 %copy-start.16 = (pred[6]{0:T(512)(128)(4,1)S(1)}, pred[6]{0:T(512)(128)(4,1)}, u32[]{:S(2)}) copy-start(pred[6]{0:T(512)(128)(4,1)} %get-tuple-element.336) | copy-start | bytes 22
  270.7 5.8 %copy-start.17 = (pred[6]{0:T(512)(128)(4,1)S(1)}, pred[6]{0:T(512)(128)(4,1)}, u32[]{:S(2)}) copy-start(pred[6]{0:T(512)(128)(4,1)} %get-tuple-element.337) | copy-start | bytes 22
  276.4 2.7 copy-start.11
  276.4 118.0 %reduce-scatter.4.cloned.1.call-start = ((), (), s32[]{:S(2)}) async-start(), calls=%async_computation.3 | async-start | bytes 589824 | tf_op jit(solution)/shard_map/reduce_scatter | solution.py:181
  279.1 5.8 %copy-start.15 = (pred[6]{0:T(512)(128)(4,1)S(1)}, pred[6]{0:T(512)(128)(4,1)}, u32[]{:S(2)}) copy-start(pred[6]{0:T(512)(128)(4,1)} %get-tuple-element.325) | copy-start | bytes 22
  284.8 2.5 copy-start.14
Sparse Core Ops, SparseCore 0:
  267.8 50.0 reduce-scatter.5
  320.6 35.5 reduce-scatter.7
  358.8 35.5 reduce-scatter.3
where the time goes:
time: 407 us; the launch traced here: 402 us
  waiting for transfers between devices  144 us (35%)
  local copies, waits for them, and re-layouts  112 us (28%)
  matrix products  47.2 us (12%)
  other arithmetic  45 us (11%)
  between operations  38.2 us (9%)
  starting transfers between devices  16.5 us (4%)
    reduce_scatter x3, waiting for transfers between devices, local(): lax.psum_scatter(projected, 'tp', scatter_dimension=2, tiled=True)  104 us
    ppermute x12, waiting for transfers between devices, passed_along(): return lax.ppermute(value, axis, pairs)  39.8 us
    scatter x15, local copies, waits for them, and re-layouts, local(): landed = landed.at[lane_number].set(lane_block)  38 us
    unnamed x71, local copies, waits for them, and re-layouts  17.7 us
    dot_general x3, matrix products, local(): jnp.dot(heads_out.reshape(slot_total * round_size, -1), out_proj, preferr...  17.2 us
    ppermute x12, starting transfers between devices, passed_along(): return lax.ppermute(value, axis, pairs)  16.4 us
    dot_general x6, matrix products, attend(): jnp.einsum('stkgd,slkd->stkgl', query_heads, keys_all[:, :, :, 0], prefer...  14.9 us
    dot_general x6, matrix products, attend(): jnp.einsum('stkgl,slkd->stkgd', cache_weight, keys_all[:, :, :, 1], prefe...  12.4 us
  transfers between devices with their start and end apart: 15, of which 5 were waited for; matrix products, arithmetic and copies ran while one was open for 34% of the time, Pallas kernels for 0%

commit v1 on v0

v1 whole, which is shorter than its diff:
```python
import functools

import jax
import jax.numpy as jnp
from jax import lax
from jax.experimental import pallas as pl
from jax.experimental.pallas import tpu as pltpu
from jax.sharding import PartitionSpec as P

MESH = pl.DeviceIdType.MESH
HEAD_DIM = 128
R_DEV = 8
LANES = 4
DISTANCES = (1, 2, 8, 16)
INSTANCES = 32
TP = 8
CACHE = 2048
PAD_KEYS = 128
STEPS = 6
GROUP = 8
COLS = 512
CHUNK = 256
CHUNKS = CACHE // CHUNK
MASKED = -1e30
SCALE = HEAD_DIM**-0.5

RELAYS = (
    (0, 15, 0, 0, 1),
    (1, 10, 14, 12, 0),
    (1, 14, 1, 0, 1),
    (1, 15, 2, 1, 1),
    (2, 0, 12, 8, 0),
)
EXTRA_PAIRS = (
    (15, 0, 0),
    (10, 14, 0),
    (14, 1, 0),
    (15, 2, 0),
    (0, 12, 0),
    (1, 0, 1),
    (2, 1, 1),
    (12, 8, 0),
)


def softmax_rows(scores):
    top = jnp.max(scores, axis=-1, keepdims=True)
    grown = jnp.exp(scores - top)
    total = jnp.sum(grown, axis=-1, keepdims=True)
    return (grown / total).astype(jnp.bfloat16)


def dot_t(a, b):
    return lax.dot_general(a, b, (((1,), (1,)), ((), ())), preferred_element_type=jnp.float32)


def kernel(
    moving_ref, destination_ref, pages_ref, lengths_ref,
    kv_hbm, q_hbm, fresh_hbm, proj_hbm,
    att_ref, cache_ref,
    kv, send, relay, proj, q_v, fresh_v,
    ask_out, ask_in, head_out, head_in, q_f, fresh_f, ask_f, heads, part_out, part_in, result, stay,
    kv_sem, load_sem, bulk_send, bulk_recv, relay_recv, relay_send,
    ask_send, ask_recv, head_send, head_recv, part_send, part_recv,
):
    me = lax.axis_index("inst")
    tp = lax.axis_index("tp")
    half = me // 16
    place = me % 16

    small_loads = [
        pltpu.make_async_copy(q_hbm, q_v, load_sem.at[0]),
        pltpu.make_async_copy(fresh_hbm, fresh_v, load_sem.at[1]),
    ]
    for copy in small_loads:
        copy.start()
    kv_load = [
        pltpu.make_async_copy(kv_hbm.at[row], kv.at[row, pl.ds(0, CACHE)], kv_sem.at[row])
        for row in range(R_DEV)
    ]
    for copy in kv_load:
        copy.start()
    proj_load = pltpu.make_async_copy(proj_hbm, proj, load_sem.at[2])
    proj_load.start()

    barrier = pltpu.get_barrier_semaphore()

    def greet(inst, peer):
        pl.semaphore_signal(barrier, inc=1, device_id=(inst, peer), device_id_type=MESH)

    for distance in (1, 2, 8, 16, 24, 30, 31):
        greet(lax.rem(me + distance, INSTANCES), tp)
    for offset in range(1, TP):
        greet(me, lax.rem(tp + offset, TP))
    greeted = jnp.int32(7 + TP - 1)
    for first, second, flip in EXTRA_PAIRS:
        other_half = (1 - half if flip else half) * 16

        @pl.when(place == first)
        def _():
            greet(other_half + second, tp)

        @pl.when(place == second)
        def _():
            greet(other_half + first, tp)

        greeted = greeted + jnp.where((place == first) | (place == second), 1, 0)

    moving = moving_ref[...]
    destination = destination_ref[...]
    source = moving >> 3
    distance_all = (destination - source) & (INSTANCES - 1)
    code = lax.broadcasted_iota(jnp.int32, moving.shape, 1) * R_DEV + (moving & (R_DEV - 1))
    own_row, own_length, own_done, arrival_done = [], [], [], []

    def done_round(m):
        return jnp.where(pages_ref[m, 2] > 0, 2, jnp.where(pages_ref[m, 1] > 0, 1, 0))

    for lane in range(LANES):
        on_lane = distance_all == DISTANCES[lane]
        own = jnp.sum(jnp.where(on_lane & (source == me), code, 0))
        arriving = jnp.sum(jnp.where(on_lane & (destination == me), code, 0))
        row = own & (R_DEV - 1)
        own_row.append(row)
        own_length.append(lengths_ref[me * R_DEV + row])
        own_done.append(done_round(own >> 3))
        arrival_done.append(done_round(arriving >> 3))
    staying, stay_place = [], []
    count = jnp.int32(0)
    for row in range(R_DEV):
        gone = own_row[0] == row
        for lane in range(1, LANES):
            gone = gone | (own_row[lane] == row)
        stays = jnp.where(gone, 0, 1)
        staying.append(stays)
        stay_place.append(count)
        count = count + stays
    for index in range(R_DEV - LANES):
        chosen = jnp.int32(0)
        for row in range(R_DEV):
            chosen = jnp.where((staying[row] == 1) & (stay_place[row] == index), row, chosen)
        stay[index] = chosen

    for copy in small_loads:
        copy.wait()
    ask_f[...] = jnp.zeros_like(ask_f)
    for lane in range(LANES):
        queries = q_v[R_DEV + lane].astype(jnp.float32)
        for head in range(GROUP):
            ask_f[2 * head : 2 * head + 2, :] = queries[4:6, head * HEAD_DIM : (head + 1) * HEAD_DIM]
        fresh = fresh_v[R_DEV + lane].astype(jnp.float32)
        ask_f[16:22, :] = fresh[:, :HEAD_DIM]
        ask_f[32:38, :] = fresh[:, HEAD_DIM:]
        ask_out[lane] = ask_f[...].astype(jnp.bfloat16)

    fresh_f[...] = jnp.zeros_like(fresh_f)
    for row in range(R_DEV):
        fresh_f[0:STEPS, :] = fresh_v[row].astype(jnp.float32)
        kv[row, CACHE : CACHE + PAD_KEYS, :] = fresh_f[...].astype(jnp.bfloat16)

    for copy in kv_load:
        copy.wait()
    for lane in range(LANES):

        def move_part(part, carry, lane=lane):
            where = pl.ds(pl.multiple_of(part * CHUNK, CHUNK), CHUNK)
            send[lane, where, :] = kv[own_row[lane], where, :]
            return carry

        lax.fori_loop(0, CHUNKS, move_part, 0)

    pl.semaphore_wait(barrier, greeted)

    def ask_copy(lane):
        return pltpu.make_async_remote_copy(
            src_ref=ask_out.at[lane], dst_ref=ask_in.at[lane],
            send_sem=ask_send.at[lane], recv_sem=ask_recv.at[lane],
            device_id=(lax.rem(me + INSTANCES - DISTANCES[lane], INSTANCES), tp), device_id_type=MESH,
        )

    def head_copy(lane):
        return pltpu.make_async_remote_copy(
            src_ref=head_out.at[lane], dst_ref=head_in.at[lane],
            send_sem=head_send.at[lane], recv_sem=head_recv.at[lane],
            device_id=(lax.rem(me + DISTANCES[lane], INSTANCES), tp), device_id_type=MESH,
        )

    def bulk_copy(lane, first, rows):
        where = pl.ds(first, rows)
        return pltpu.make_async_remote_copy(
            src_ref=send.at[lane, where], dst_ref=cache_ref.at[lane, where],
            send_sem=bulk_send.at[lane], recv_sem=bulk_recv.at[lane],
            device_id=(lax.rem(me + DISTANCES[lane], INSTANCES), tp), device_id_type=MESH,
        )

    special = [jnp.int32(0) for _ in range(LANES)]
    relay_of = [me for _ in range(LANES)]
    is_relay = jnp.int32(0)
    relay_lane = jnp.int32(0)
    relay_final = me
    for lane, first, middle, final, flip in RELAYS:
        special[lane] = jnp.where(place == first, 1, special[lane])
        relay_of[lane] = jnp.where(place == first, half * 16 + middle, relay_of[lane])
        is_relay = jnp.where(place == middle, 1, is_relay)
        relay_lane = jnp.where(place == middle, lane, relay_lane)
        last = (1 - half if flip else half) * 16 + final
        relay_final = jnp.where(place == middle, last, relay_final)
    relayed_lanes = sorted({entry[0] for entry in RELAYS})

    def first_leg(lane, chunk):
        where = pl.ds(chunk * CHUNK, CHUNK)
        return pltpu.make_async_remote_copy(
            src_ref=send.at[lane, where], dst_ref=relay.at[where],
            send_sem=bulk_send.at[lane], recv_sem=relay_recv.at[chunk],
            device_id=(relay_of[lane], tp), device_id_type=MESH,
        )

    def second_leg(chunk):
        where = pl.ds(chunk * CHUNK, CHUNK)
        return pltpu.make_async_remote_copy(
            src_ref=relay.at[where], dst_ref=cache_ref.at[relay_lane, where],
            send_sem=relay_send.at[chunk], recv_sem=bulk_recv.at[relay_lane],
            device_id=(relay_final, tp), device_id_type=MESH,
        )

    def start_lane(lane, chunk):
        if lane in relayed_lanes:

            @pl.when(special[lane] == 1)
            def _():
                first_leg(lane, chunk).start()

            @pl.when(special[lane] == 0)
            def _():
                bulk_copy(lane, chunk * CHUNK, CHUNK).start()

        else:
            bulk_copy(lane, chunk * CHUNK, CHUNK).start()

    def forward(chunks):
        @pl.when(is_relay == 1)
        def _():
            for chunk in chunks:
                where = pl.ds(chunk * CHUNK, CHUNK)
                pltpu.make_async_remote_copy(
                    src_ref=relay.at[where], dst_ref=relay.at[where],
                    send_sem=relay_send.at[chunk], recv_sem=relay_recv.at[chunk],
                    device_id=(relay_final, tp), device_id_type=MESH,
                ).wait_recv()
                second_leg(chunk).start()

    for lane in range(LANES):
        ask_copy(lane).start()
    for chunk in range(CHUNKS - 1):
        for lane in range(LANES):
            start_lane(lane, chunk)

    position = lax.broadcasted_iota(jnp.int32, (CHUNK, 1), 0) + (CACHE - CHUNK)
    for lane in range(LANES):
        ask_copy(lane).wait_recv()
        fresh_key = ask_in[lane, 16:32, :].astype(jnp.float32)
        fresh_value = ask_in[lane, 32:48, :].astype(jnp.float32)
        length = own_length[lane]
        decodes = own_done[lane] < 2
        old = send[lane, CACHE - CHUNK : CACHE, :].astype(jnp.float32)
        for part, fresh in ((0, fresh_key), (1, fresh_value)):
            columns = slice(part * HEAD_DIM, (part + 1) * HEAD_DIM)
            new = jnp.where(position < length, old[:, columns], 0.0)
            new = jnp.where((position == length) & decodes, fresh[4:5, :], new)
            new = jnp.where((position == length + 1) & decodes, fresh[5:6, :], new)
            send[lane, CACHE - CHUNK : CACHE, columns] = new.astype(jnp.bfloat16)
        start_lane(lane, CHUNKS - 1)

    for lane in range(LANES):
        scores = dot_t(ask_in[lane, 0:16, :], send[lane, :, :HEAD_DIM]) * SCALE
        key_at = lax.broadcasted_iota(jnp.int32, scores.shape, 1)
        step = lax.broadcasted_iota(jnp.int32, scores.shape, 0) & 1
        scores = jnp.where(key_at <= own_length[lane] + step, scores, MASKED)
        mixed = jnp.dot(softmax_rows(scores), send[lane, :, HEAD_DIM:], preferred_element_type=jnp.float32)
        head_out[lane] = mixed.astype(jnp.bfloat16)
        head_copy(lane).start()

    forward(range(0, 2))

    q_f[...] = jnp.zeros_like(q_f)

    def home(index, carry):
        row = stay[index]
        length = lengths_ref[me * R_DEV + row]
        queries = q_v[row].astype(jnp.float32)
        for head in range(GROUP):
            q_f[8 * head : 8 * head + STEPS, :] = queries[:, head * HEAD_DIM : (head + 1) * HEAD_DIM]
        scores = dot_t(q_f[...].astype(jnp.bfloat16), kv[row, :, :HEAD_DIM]) * SCALE
        key_at = lax.broadcasted_iota(jnp.int32, scores.shape, 1)
        step = lax.broadcasted_iota(jnp.int32, scores.shape, 0) & 7
        seen = (key_at < length) | ((key_at >= CACHE) & (key_at - CACHE <= step))
        scores = jnp.where(seen, scores, MASKED)
        mixed = jnp.dot(softmax_rows(scores), kv[row, :, HEAD_DIM:], preferred_element_type=jnp.float32)
        for head in range(GROUP):
            heads[index, 0:STEPS, head * HEAD_DIM : (head + 1) * HEAD_DIM] = mixed[8 * head : 8 * head + STEPS, :]
        return carry

    lax.fori_loop(0, R_DEV - LANES, home, 0)

    forward(range(2, 5))

    for lane in range(LANES):
        head_copy(lane).wait_recv()
        arrived = head_in[lane].astype(jnp.float32)
        for head in range(GROUP):
            heads[lane, STEPS : STEPS + 2, head * HEAD_DIM : (head + 1) * HEAD_DIM] = arrived[2 * head : 2 * head + 2, :]

    proj_load.wait()
    rows = heads[...].reshape(R_DEV * LANES, GROUP * HEAD_DIM).astype(jnp.bfloat16)

    def part_copy(peer, slot):
        return pltpu.make_async_remote_copy(
            src_ref=part_out.at[peer], dst_ref=part_in.at[slot],
            send_sem=part_send.at[peer], recv_sem=part_recv.at[slot],
            device_id=(me, peer), device_id_type=MESH,
        )

    def project(peer):
        columns = pl.ds(pl.multiple_of(peer * COLS, COLS), COLS)
        return jnp.dot(rows, proj[:, columns], preferred_element_type=jnp.float32)

    def project_for(offset, carry):
        peer = lax.rem(tp + offset, TP)
        part_out[peer] = project(peer).astype(jnp.bfloat16)
        part_copy(peer, tp).start()
        return carry

    lax.fori_loop(1, TP, project_for, 0)
    total = project(tp)

    forward(range(5, CHUNKS))

    for offset in range(1, TP):
        peer = lax.rem(tp + offset, TP)
        part_copy(peer, peer).wait_recv()
        total = total + part_in[peer].astype(jnp.float32)
    result[...] = total.reshape(LANES, R_DEV, COLS)

    for row in range(R_DEV):
        found = result[jnp.minimum(stay_place[row], R_DEV - LANES - 1)]
        att_ref[row] = jnp.where(staying[row] == 1, found[0:STEPS, :], 0.0).astype(jnp.bfloat16)
    for lane in range(LANES):
        found = jnp.concatenate([jnp.zeros((4, COLS), jnp.float32), result[lane, STEPS : STEPS + 2, :]], axis=0)
        att_ref[R_DEV + lane] = jnp.where(arrival_done[lane] < 2, found, 0.0).astype(jnp.bfloat16)

    for lane in range(LANES):
        ask_copy(lane).wait_send()
        head_copy(lane).wait_send()
        bulk_copy(lane, 0, CACHE).wait_send()
    for offset in range(1, TP):
        part_copy(lax.rem(tp + offset, TP), tp).wait_send()

    @pl.when(is_relay == 1)
    def _():
        for chunk in range(CHUNKS):
            second_leg(chunk).wait_send()

    for lane in range(LANES):
        bulk_copy(lane, 0, CACHE).wait_recv()


def local(kv_cache, queries, fresh_kv, out_proj, moving, destination, round_pages, lengths):
    bf16, f32 = jnp.bfloat16, jnp.float32
    row_width = kv_cache.shape[2]
    dma = pltpu.SemaphoreType.DMA
    any_space = pl.BlockSpec(memory_space=pl.ANY)
    smem = pl.BlockSpec(memory_space=pltpu.SMEM)
    vmem = pl.BlockSpec(memory_space=pltpu.VMEM)
    slots = R_DEV + LANES
    attended, arrived = pl.pallas_call(
        kernel,
        out_shape=(
            jax.ShapeDtypeStruct((slots, STEPS, COLS), bf16),
            jax.ShapeDtypeStruct((LANES, CACHE, row_width), bf16),
        ),
        in_specs=[vmem, vmem, smem, smem, any_space, any_space, any_space, any_space],
        out_specs=(vmem, any_space),
        scratch_shapes=[
            pltpu.VMEM((R_DEV, CACHE + PAD_KEYS, row_width), bf16),
            pltpu.VMEM((LANES, CACHE, row_width), bf16),
            pltpu.VMEM((CACHE, row_width), bf16),
            pltpu.VMEM(out_proj.shape, bf16),
            pltpu.VMEM(queries.shape, bf16),
            pltpu.VMEM(fresh_kv.shape, bf16),
            pltpu.VMEM((LANES, 48, HEAD_DIM), bf16),
            pltpu.VMEM((LANES, 48, HEAD_DIM), bf16),
            pltpu.VMEM((LANES, 16, HEAD_DIM), bf16),
            pltpu.VMEM((LANES, 16, HEAD_DIM), bf16),
            pltpu.VMEM((8 * GROUP, HEAD_DIM), f32),
            pltpu.VMEM((PAD_KEYS, row_width), f32),
            pltpu.VMEM((48, HEAD_DIM), f32),
            pltpu.VMEM((LANES, R_DEV, GROUP * HEAD_DIM), f32),
            pltpu.VMEM((TP, LANES * R_DEV, COLS), bf16),
            pltpu.VMEM((TP, LANES * R_DEV, COLS), bf16),
            pltpu.VMEM((LANES, R_DEV, COLS), f32),
            pltpu.SMEM((R_DEV - LANES,), jnp.int32),
            dma((R_DEV,)),
            dma((3,)),
            dma((LANES,)),
            dma((LANES,)),
            dma((CHUNKS,)),
            dma((CHUNKS,)),
            dma((LANES,)),
            dma((LANES,)),
            dma((LANES,)),
            dma((LANES,)),
            dma((TP,)),
            dma((TP,)),
        ],
        compiler_params=pltpu.CompilerParams(
            collective_id=0, has_side_effects=True, vmem_limit_bytes=48 * 2**20
        ),
    )(
        moving.reshape(1, -1), destination.reshape(1, -1), round_pages, lengths,
        kv_cache, queries, fresh_kv, out_proj,
    )
    return attended, arrived


def solution(mesh):
    in_specs = (
        P("inst", None, "tp"),
        P("inst", None, "tp"),
        P("inst", None, "tp"),
        P("tp", None),
        P(),
        P(),
        P(),
        P(),
    )
    out_specs = (P("inst", None, "tp"), P("inst", None, "tp"))
    return jax.shard_map(local, mesh=mesh, in_specs=in_specs, out_specs=out_specs, check_vma=False)
```

time: 407 us -> 93.6 us (0.23); the launches traced: 402 us -> 93.4 us
  waiting for transfers between devices: 144 us -> 0 us
  local copies, waits for them, and re-layouts: 112 us -> 7.15 us
  Pallas kernels: 0 us -> 85.6 us
  matrix products: 47.2 us -> 0 us
  other arithmetic: 45 us -> 0 us
  between operations: 38.2 us -> 0.65 us
  starting transfers between devices: 16.5 us -> 0 us
    reduce_scatter x3 -> x0, waiting for transfers between devices: 104 us -> none  [local(): lax.psum_scatter(projected, 'tp', scatter_dimension=2, tiled=True)]
    pallas_call x0 -> x1, Pallas kernels: none -> 85.6 us  [local(): pl.pallas_call(kernel, out_shape=(jax.ShapeDtypeStruct((slots, STEPS, COL...]
    dot_general x27 -> x0, matrix products: 47.2 us -> none  [the longest x3 17.2 us: local(): jnp.dot(heads_out.reshape(slot_total * round_size, -1), out_proj, preferr...]
    scatter x19 -> x0, local copies, waits for them, and re-layouts: 42.1 us -> none  [the longest x15 38 us: local(): landed = landed.at[lane_number].set(lane_block)]
    ppermute x12 -> x0, waiting for transfers between devices: 39.8 us -> none  [passed_along(): return lax.ppermute(value, axis, pairs)]
    slice x31 -> x0, local copies, waits for them, and re-layouts: 29.6 us -> none  [the longest x10 10.9 us: local(): landed[lane_number]]
    select_n x12 -> x0, other arithmetic: 19.1 us -> none  [the longest x5 10.6 us: local(): jnp.where((jnp.arange(span_rows) < own_pages[lane_number, round_number] *...]
    ppermute x12 -> x0, starting transfers between devices: 16.4 us -> none  [passed_along(): return lax.ppermute(value, axis, pairs)]
  transfers between devices with their start and end apart: 15 -> 0, of which waited for: 5 -> 0; matrix products, arithmetic and copies ran while one was open for 34% -> 0% of each run, Pallas kernels for 0% -> 0%
where the time goes in v1:
time: 93.6 us; the launch traced here: 93.4 us
  Pallas kernels  85.6 us (91%)
  local copies, waits for them, and re-layouts  7.15 us (8%)
    pallas_call x1, Pallas kernels, local(): pl.pallas_call(kernel, out_shape=(jax.ShapeDtypeStruct((slots, STEPS, COL...  85.6 us
    unnamed x13, local copies, waits for them, and re-layouts  7.15 us

profile of v1, /device:TPU:1, one launch (start us, length us, event | category | flops | bytes accessed | tf_op | source)
XLA Modules:
  0.0 93.4 jit_solution(6176134744673637926)
XLA Ops:
  0.6 0.8 copy.10.pages_ref
  1.4 0.0 copy-start
  1.4 0.9 copy-done
  2.3 0.0 copy-start.1
  2.3 0.8 copy-done.1
  3.1 0.0 copy-start.2
  3.1 0.7 copy-done.2
  3.8 0.0 copy-start.3
  3.8 0.7 copy-done.3
  4.5 0.0 copy-start.4
  4.5 0.7 copy-done.4
  5.1 85.6 %shard_map.95 = (bf16[12,6,512]{2,1,0:T(8,128)(2,1)S(1)}, bf16[4,2048,256]{2,1,0:T(8,128)(2,1)S(1)}) custom-call(s32[1,128]{1,0:T(1,128)S(1)} %bitcast.2, s32[1,128]{1,0:T(1,128)S(1)} %bitcast.3, s32[128,3]{1,0:T(8,128)S(1)} %copy.10.pages_ref, s32[256]{0:T(256)S(1)} %copy-done.2, bf16[8,2048,256]{2,1,0:T(8,128)(2,1)} %kv_hbm.1, ...), custom_call_target="tpu_custom_call" | custom-call | tf_op jit(solution)/shard_map/pallas_call | solution.py:375
  90.7 0.6 copy.13
  91.4 2.0 %copy.14 = bf16[4,2048,256]{2,1,0:T(8,128)(2,1)} copy(bf16[4,2048,256]{2,1,0:T(8,128)(2,1)S(1)} %get-tuple-element.5) | data formatting | bytes 8388608
Async XLA Ops:
  1.4 0.9 copy-start
  2.3 0.8 copy-start.1
  3.1 0.7 copy-start.2
  3.8 0.7 copy-start.3
  4.5 0.7 copy-start.4

commit v2 on v1

v2 whole, which is shorter than its diff:
```python
import functools

import jax
import jax.numpy as jnp
from jax import lax
from jax.experimental import pallas as pl
from jax.experimental.pallas import tpu as pltpu
from jax.sharding import PartitionSpec as P

MESH = pl.DeviceIdType.MESH
HEAD_DIM = 128
R_DEV = 8
LANES = 4
DISTANCES = (1, 2, 8, 16)
INSTANCES = 32
TP = 8
CACHE = 2048
PAD_KEYS = 128
STEPS = 6
GROUP = 8
COLS = 512
CHUNK = 128
CHUNKS = CACHE // CHUNK
TAIL = 256
DEPTH = 3
LAG = 5
HOPS = (2, 1, 3, 0)
PACE = ((3, 3), (3, 4), (4, 4), (4, 5), (5, 6), (6, 6), (6, 7), (7, 8), (8, 8), (8, 8), (8, 9), (9, 9), (9, 9), (9, 10), (10, 10), (10, 10), (10, 11), (11, 16))
MASKED = -1e30
SCALE = HEAD_DIM**-0.5

RELAYS = (
    (0, 15, 0, 0, 0, 12),
    (1, 0, 3, 0, 0, 4),
    (1, 2, 6, 0, 0, 8),
    (1, 4, 7, 0, 0, 4),
    (1, 6, 10, 0, 0, 12),
    (1, 8, 11, 0, 0, 4),
    (1, 10, 9, 0, 0, 8),
    (1, 10, 14, 0, 8, 16),
    (1, 12, 15, 0, 0, 4),
    (1, 14, 1, 0, 0, 12),
    (1, 15, 2, 0, 0, 12),
    (2, 0, 12, 0, 0, 12),
    (2, 1, 13, 0, 0, 4),
    (2, 8, 4, 0, 0, 12),
    (2, 9, 5, 0, 0, 4),
    (2, 10, 6, 0, 0, 4),
    (2, 11, 3, 0, 0, 4),
    (2, 12, 8, 0, 0, 4),
    (2, 13, 5, 0, 0, 4),
    (2, 14, 6, 0, 0, 8),
    (2, 15, 7, 0, 0, 12),
)


def relay_plan():
    plan, slots = {}, {}
    for lane, source, middle, flip, first, last in RELAYS:
        for chunk in range(first, last):
            plan.setdefault(middle, []).append((chunk * CHUNK, lane, source, flip))
    for middle in plan:
        plan[middle].sort()
        for slot, (row, lane, source, flip) in enumerate(plan[middle]):
            slots[middle, lane, source, row] = slot
    base = {(d, 0) for d in DISTANCES} | {(INSTANCES - d, 0) for d in DISTANCES}
    pairs = []

    def meet(first, second, flip):
        shift_a = (second + 16 * flip - first) % INSTANCES
        shift_b = (second - first - 16 * flip) % INSTANCES
        known = all((shift, 0) in base for shift in (shift_a, shift_b))
        entry, back = (first, second, flip), (second, first, flip)
        if not known and entry not in pairs and back not in pairs:
            pairs.append(entry)

    for lane, source, middle, flip, first, last in RELAYS:
        meet(source, middle, flip)
        final = source + DISTANCES[lane]
        meet(middle, final % 16, (flip + final // 16) % 2)
    return plan, slots, tuple(pairs)


RELAY_PLAN, RELAY_SLOTS, EXTRA_PAIRS = relay_plan()
RELAY_PIECES = max([len(pieces) for pieces in RELAY_PLAN.values()], default=1)


def softmax_rows(scores):
    top = jnp.max(scores, axis=-1, keepdims=True)
    grown = jnp.exp(scores - top)
    total = jnp.sum(grown, axis=-1, keepdims=True)
    return (grown * (1.0 / total)).astype(jnp.bfloat16)


def dot_t(a, b):
    return lax.dot_general(a, b, (((1,), (1,)), ((), ())), preferred_element_type=jnp.float32)


def kernel(
    moving_hbm, destination_hbm, pages_hbm, lengths_hbm,
    kv_hbm, q_hbm, fresh_hbm, proj_hbm,
    att_ref, cache_ref,
    kv, send, relay, proj, q_v, fresh_v,
    moving_ref, destination_ref, pages_ref, lengths_ref,
    ask_out, ask_in, head_out, head_in, q_f, fresh_f, ask_f, heads, pair_out, pair_in, part_out, part_in, result, stay,
    kv_sem, load_sem, bulk_send, bulk_recv, relay_recv, relay_send,
    ask_send, ask_recv, head_send, head_recv, pair_send, pair_recv, part_send, part_recv,
):
    me = lax.axis_index("inst")
    tp = lax.axis_index("tp")
    half = me // 16
    place = me % 16

    plan_loads = [
        pltpu.make_async_copy(moving_hbm, moving_ref, load_sem.at[3]),
        pltpu.make_async_copy(destination_hbm, destination_ref, load_sem.at[4]),
        pltpu.make_async_copy(pages_hbm, pages_ref, load_sem.at[5]),
        pltpu.make_async_copy(lengths_hbm, lengths_ref, load_sem.at[6]),
    ]
    small_loads = [
        pltpu.make_async_copy(q_hbm, q_v, load_sem.at[0]),
        pltpu.make_async_copy(fresh_hbm, fresh_v, load_sem.at[1]),
    ]
    kv_load = [
        pltpu.make_async_copy(kv_hbm.at[row], kv.at[row, pl.ds(0, CACHE)], kv_sem.at[row])
        for row in range(R_DEV)
    ]
    proj_load = pltpu.make_async_copy(proj_hbm, proj, load_sem.at[2])
    for copy in plan_loads + small_loads + kv_load:
        copy.start()

    barrier = pltpu.get_barrier_semaphore()

    def greet(inst, peer):
        pl.semaphore_signal(barrier, inc=1, device_id=(inst, peer), device_id_type=MESH)

    for distance in (1, 2, 8, 16, 24, 30, 31):
        greet(lax.rem(me + distance, INSTANCES), tp)
    core = tp % 2
    sibling = tp + 1 - 2 * core
    greet(me, sibling)
    for hop in range(1, TP // 2):
        greet(me, lax.rem(tp + 2 * hop, TP))
    greeted = jnp.int32(7 + TP // 2)
    for first, second, flip in EXTRA_PAIRS:
        other_half = (1 - half if flip else half) * 16

        @pl.when(place == first)
        def _():
            greet(other_half + second, tp)

        @pl.when(place == second)
        def _():
            greet(other_half + first, tp)

        greeted = greeted + jnp.where((place == first) | (place == second), 1, 0)

    for copy in plan_loads:
        copy.wait()
    moving = moving_ref[...]
    destination = destination_ref[...]
    source = moving >> 3
    distance_all = (destination - source) & (INSTANCES - 1)
    code = lax.broadcasted_iota(jnp.int32, moving.shape, 1) * R_DEV + (moving & (R_DEV - 1))
    own_row, own_length, own_done, arrival_done = [], [], [], []

    def done_round(m):
        return jnp.where(pages_ref[2, m] > 0, 2, jnp.where(pages_ref[1, m] > 0, 1, 0))

    for lane in range(LANES):
        on_lane = distance_all == DISTANCES[lane]
        own = jnp.sum(jnp.where(on_lane & (source == me), code, 0))
        arriving = jnp.sum(jnp.where(on_lane & (destination == me), code, 0))
        row = own & (R_DEV - 1)
        own_row.append(row)
        own_length.append(lengths_ref[me * R_DEV + row])
        own_done.append(done_round(own >> 3))
        arrival_done.append(done_round(arriving >> 3))
    staying, stay_place = [], []
    count = jnp.int32(0)
    for row in range(R_DEV):
        gone = own_row[0] == row
        for lane in range(1, LANES):
            gone = gone | (own_row[lane] == row)
        stays = jnp.where(gone, 0, 1)
        staying.append(stays)
        stay_place.append(count)
        count = count + stays
    for index in range(R_DEV - LANES):
        chosen = jnp.int32(0)
        for row in range(R_DEV):
            chosen = jnp.where((staying[row] == 1) & (stay_place[row] == index), row, chosen)
        stay[index] = chosen

    for copy in small_loads:
        copy.wait()
    ask_f[...] = jnp.zeros_like(ask_f)
    for lane in range(LANES):
        queries = q_v[R_DEV + lane].astype(jnp.float32)
        for head in range(GROUP):
            ask_f[2 * head : 2 * head + 2, :] = queries[4:6, head * HEAD_DIM : (head + 1) * HEAD_DIM]
        fresh = fresh_v[R_DEV + lane].astype(jnp.float32)
        ask_f[16:22, :] = fresh[:, :HEAD_DIM]
        ask_f[32:38, :] = fresh[:, HEAD_DIM:]
        ask_out[lane] = ask_f[...].astype(jnp.bfloat16)

    for copy in kv_load:
        copy.wait()
    for lane in range(LANES):

        def move_part(part, carry, lane=lane):
            where = pl.ds(pl.multiple_of(part * TAIL, TAIL), TAIL)
            send[lane, where, :] = kv[own_row[lane], where, :]
            return carry

        lax.fori_loop(0, CACHE // TAIL, move_part, 0)

    pl.semaphore_wait(barrier, greeted)

    def ask_copy(lane):
        return pltpu.make_async_remote_copy(
            src_ref=ask_out.at[lane], dst_ref=ask_in.at[lane],
            send_sem=ask_send.at[lane], recv_sem=ask_recv.at[lane],
            device_id=(lax.rem(me + INSTANCES - DISTANCES[lane], INSTANCES), tp), device_id_type=MESH,
        )

    def head_copy(lane):
        return pltpu.make_async_remote_copy(
            src_ref=head_out.at[lane], dst_ref=head_in.at[lane],
            send_sem=head_send.at[lane], recv_sem=head_recv.at[lane],
            device_id=(lax.rem(me + DISTANCES[lane], INSTANCES), tp), device_id_type=MESH,
        )

    def bulk_copy(lane, first, rows):
        where = pl.ds(first, rows)
        return pltpu.make_async_remote_copy(
            src_ref=send.at[lane, where], dst_ref=cache_ref.at[lane, where],
            send_sem=bulk_send.at[lane, first // CHUNK], recv_sem=bulk_recv.at[lane],
            device_id=(lax.rem(me + DISTANCES[lane], INSTANCES), tp), device_id_type=MESH,
        )

    def first_leg(lane, source, middle, flip, row):
        slot = RELAY_SLOTS[middle, lane, source, row]
        return pltpu.make_async_remote_copy(
            src_ref=send.at[lane, pl.ds(row, CHUNK)], dst_ref=relay.at[pl.ds(slot * CHUNK, CHUNK)],
            send_sem=bulk_send.at[lane, row // CHUNK], recv_sem=relay_recv.at[slot],
            device_id=((1 - half if flip else half) * 16 + middle, tp), device_id_type=MESH,
        )

    def second_leg(slot, row, lane, source, flip):
        origin = (1 - half if flip else half) * 16 + source
        return pltpu.make_async_remote_copy(
            src_ref=relay.at[pl.ds(slot * CHUNK, CHUNK)], dst_ref=cache_ref.at[lane, pl.ds(row, CHUNK)],
            send_sem=relay_send.at[slot], recv_sem=bulk_recv.at[lane],
            device_id=(lax.rem(origin + DISTANCES[lane], INSTANCES), tp), device_id_type=MESH,
        )

    def landed(slot):
        piece = relay.at[pl.ds(slot * CHUNK, CHUNK)]
        return pltpu.make_async_remote_copy(
            src_ref=piece, dst_ref=piece, send_sem=relay_send.at[slot], recv_sem=relay_recv.at[slot],
            device_id=(lax.rem(me + 1, INSTANCES), tp), device_id_type=MESH,
        )

    def start_lane(lane, chunk):
        direct = None
        for relayed, source, middle, flip, first, last in RELAYS:
            if relayed == lane and first <= chunk < last:

                @pl.when(place == source)
                def _():
                    first_leg(lane, source, middle, flip, chunk * CHUNK).start()

                here = place != source
                direct = here if direct is None else direct & here
        if direct is None:
            bulk_copy(lane, chunk * CHUNK, CHUNK).start()
        else:

            @pl.when(direct)
            def _():
                bulk_copy(lane, chunk * CHUNK, CHUNK).start()

    def forward(chunk):
        for middle, pieces in RELAY_PLAN.items():
            due = [slot for slot in range(len(pieces)) if pieces[slot][0] == chunk * CHUNK]
            if due:

                @pl.when(place == middle)
                def _():
                    for slot in due:
                        landed(slot).wait_recv()
                        second_leg(slot, *pieces[slot]).start()

    def migrate(first, last):
        for step in range(first, last):
            if step < CHUNKS:
                for lane in range(LANES):
                    if step >= DEPTH:
                        bulk_copy(lane, (step - DEPTH) * CHUNK, CHUNK).wait_send()
                    start_lane(lane, step)
            if step >= LAG:
                forward(step - LAG)

    for lane in range(LANES):
        ask_copy(lane).start()
    migrate(0, DEPTH)
    proj_load.start()

    position = lax.broadcasted_iota(jnp.int32, (TAIL, 1), 0) + (CACHE - TAIL)
    for lane in range(LANES):
        ask_copy(lane).wait_recv()
        fresh_key = ask_in[lane, 16:32, :].astype(jnp.float32)
        fresh_value = ask_in[lane, 32:48, :].astype(jnp.float32)
        length = own_length[lane]
        decodes = own_done[lane] < 2
        old = send[lane, CACHE - TAIL : CACHE, :].astype(jnp.float32)
        for part, fresh in ((0, fresh_key), (1, fresh_value)):
            columns = slice(part * HEAD_DIM, (part + 1) * HEAD_DIM)
            new = jnp.where(position < length, old[:, columns], 0.0)
            new = jnp.where((position == length) & decodes, fresh[4:5, :], new)
            new = jnp.where((position == length + 1) & decodes, fresh[5:6, :], new)
            send[lane, CACHE - TAIL : CACHE, columns] = new.astype(jnp.bfloat16)

    for lane in range(LANES):
        scores = dot_t(ask_in[lane, 0:16, :], send[lane, :, :HEAD_DIM]) * SCALE
        key_at = lax.broadcasted_iota(jnp.int32, scores.shape, 1)
        step = lax.broadcasted_iota(jnp.int32, scores.shape, 0) & 1
        scores = jnp.where(key_at <= own_length[lane] + step, scores, MASKED)
        mixed = jnp.dot(softmax_rows(scores), send[lane, :, HEAD_DIM:], preferred_element_type=jnp.float32)
        head_out[lane] = mixed.astype(jnp.bfloat16)
        head_copy(lane).start()
        migrate(*PACE[lane])

    fresh_f[...] = jnp.zeros_like(fresh_f)
    for row in range(R_DEV):
        fresh_f[0:STEPS, :] = fresh_v[row].astype(jnp.float32)
        kv[row, CACHE : CACHE + PAD_KEYS, :] = fresh_f[...].astype(jnp.bfloat16)

    q_f[...] = jnp.zeros_like(q_f)

    def home(index):
        row = stay[index]
        length = lengths_ref[me * R_DEV + row]
        queries = q_v[row].astype(jnp.float32)
        for head in range(GROUP):
            q_f[8 * head : 8 * head + STEPS, :] = queries[:, head * HEAD_DIM : (head + 1) * HEAD_DIM]
        scores = dot_t(q_f[...].astype(jnp.bfloat16), kv[row, :, :HEAD_DIM]) * SCALE
        key_at = lax.broadcasted_iota(jnp.int32, scores.shape, 1)
        step = lax.broadcasted_iota(jnp.int32, scores.shape, 0) & 7
        seen = (key_at < length) | ((key_at >= CACHE) & (key_at - CACHE <= step))
        scores = jnp.where(seen, scores, MASKED)
        mixed = jnp.dot(softmax_rows(scores), kv[row, :, HEAD_DIM:], preferred_element_type=jnp.float32)
        for head in range(GROUP):
            heads[index, 0:STEPS, head * HEAD_DIM : (head + 1) * HEAD_DIM] = mixed[8 * head : 8 * head + STEPS, :]

    for index in range(R_DEV - LANES):
        home(index)
        migrate(*PACE[4 + index])

    migrate(*PACE[8])
    for lane in range(LANES):
        head_copy(lane).wait_recv()
        arrived = head_in[lane].astype(jnp.float32)
        for head in range(GROUP):
            heads[lane, STEPS : STEPS + 2, head * HEAD_DIM : (head + 1) * HEAD_DIM] = arrived[2 * head : 2 * head + 2, :]

    proj_load.wait()
    rows = heads[...].reshape(R_DEV * LANES, GROUP * HEAD_DIM).astype(jnp.bfloat16)

    def pair_copy(hop):
        return pltpu.make_async_remote_copy(
            src_ref=pair_out.at[hop], dst_ref=pair_in.at[hop],
            send_sem=pair_send.at[hop], recv_sem=pair_recv.at[hop],
            device_id=(me, sibling), device_id_type=MESH,
        )

    def part_copy(hop):
        return pltpu.make_async_remote_copy(
            src_ref=part_out.at[hop], dst_ref=part_in.at[hop],
            send_sem=part_send.at[hop], recv_sem=part_recv.at[hop],
            device_id=(me, lax.rem(tp + 2 * hop, TP)), device_id_type=MESH,
        )

    def project(peer):
        columns = pl.ds(pl.multiple_of(peer * COLS, COLS), COLS)
        return jnp.dot(rows, proj[:, columns], preferred_element_type=jnp.float32)

    for index, hop in enumerate(HOPS):
        pair_out[hop] = project(lax.rem(sibling + 2 * hop, TP))
        pair_copy(hop).start()
        migrate(*PACE[9 + index])
    total = None
    for index, hop in enumerate(HOPS):
        mine = project(lax.rem(tp + 2 * hop, TP))
        pair_copy(hop).wait_recv()
        mine = mine + pair_in[hop]
        if hop:
            part_out[hop] = mine.astype(jnp.bfloat16)
            part_copy(hop).start()
        else:
            total = mine
        migrate(*PACE[13 + index])

    migrate(*PACE[17])
    for hop in HOPS[:-1]:
        part_copy(hop).wait_recv()
        total = total + part_in[hop].astype(jnp.float32)
    result[...] = total.reshape(LANES, R_DEV, COLS)

    for row in range(R_DEV):
        found = result[jnp.minimum(stay_place[row], R_DEV - LANES - 1)]
        att_ref[row] = jnp.where(staying[row] == 1, found[0:STEPS, :], 0.0).astype(jnp.bfloat16)
    for lane in range(LANES):
        found = jnp.concatenate([jnp.zeros((4, COLS), jnp.float32), result[lane, STEPS : STEPS + 2, :]], axis=0)
        att_ref[R_DEV + lane] = jnp.where(arrival_done[lane] < 2, found, 0.0).astype(jnp.bfloat16)

    migrate(PACE[17][1], CHUNKS + LAG)

    for lane in range(LANES):
        ask_copy(lane).wait_send()
        head_copy(lane).wait_send()
        for chunk in range(CHUNKS - DEPTH, CHUNKS):
            bulk_copy(lane, chunk * CHUNK, CHUNK).wait_send()
    for hop in HOPS:
        pair_copy(hop).wait_send()
        if hop:
            part_copy(hop).wait_send()

    for middle, pieces in RELAY_PLAN.items():

        @pl.when(place == middle)
        def _():
            for slot, piece in enumerate(pieces):
                second_leg(slot, *piece).wait_send()

    for lane in range(LANES):
        bulk_copy(lane, 0, CACHE).wait_recv()


def local(kv_cache, queries, fresh_kv, out_proj, moving, destination, round_pages, lengths):
    bf16, f32 = jnp.bfloat16, jnp.float32
    row_width = kv_cache.shape[2]
    dma = pltpu.SemaphoreType.DMA
    hbm = pl.BlockSpec(memory_space=pltpu.HBM)
    vmem = pl.BlockSpec(memory_space=pltpu.VMEM)
    slots = R_DEV + LANES
    attended, arrived = pl.pallas_call(
        kernel,
        out_shape=(
            pltpu.VMEM((slots, STEPS, COLS), bf16),
            pltpu.VMEM((LANES, CACHE, row_width), bf16),
        ),
        in_specs=[hbm] * 8,
        out_specs=(vmem, vmem),
        scratch_shapes=[
            pltpu.VMEM((R_DEV, CACHE + PAD_KEYS, row_width), bf16),
            pltpu.VMEM((LANES, CACHE, row_width), bf16),
            pltpu.VMEM((RELAY_PIECES * CHUNK, row_width), bf16),
            pltpu.VMEM(out_proj.shape, bf16),
            pltpu.VMEM(queries.shape, bf16),
            pltpu.VMEM(fresh_kv.shape, bf16),
            pltpu.VMEM((1, moving.shape[0]), jnp.int32),
            pltpu.VMEM((1, moving.shape[0]), jnp.int32),
            pltpu.SMEM((round_pages.shape[1], round_pages.shape[0]), jnp.int32),
            pltpu.SMEM(lengths.shape, jnp.int32),
            pltpu.VMEM((LANES, 48, HEAD_DIM), bf16),
            pltpu.VMEM((LANES, 48, HEAD_DIM), bf16),
            pltpu.VMEM((LANES, 16, HEAD_DIM), bf16),
            pltpu.VMEM((LANES, 16, HEAD_DIM), bf16),
            pltpu.VMEM((8 * GROUP, HEAD_DIM), f32),
            pltpu.VMEM((PAD_KEYS, row_width), f32),
            pltpu.VMEM((48, HEAD_DIM), f32),
            pltpu.VMEM((LANES, R_DEV, GROUP * HEAD_DIM), f32),
            pltpu.VMEM((TP // 2, LANES * R_DEV, COLS), f32),
            pltpu.VMEM((TP // 2, LANES * R_DEV, COLS), f32),
            pltpu.VMEM((TP // 2, LANES * R_DEV, COLS), bf16),
            pltpu.VMEM((TP // 2, LANES * R_DEV, COLS), bf16),
            pltpu.VMEM((LANES, R_DEV, COLS), f32),
            pltpu.SMEM((R_DEV - LANES,), jnp.int32),
            dma((R_DEV,)),
            dma((7,)),
            dma((LANES, CHUNKS)),
            dma((LANES,)),
            dma((RELAY_PIECES,)),
            dma((RELAY_PIECES,)),
            dma((LANES,)),
            dma((LANES,)),
            dma((LANES,)),
            dma((LANES,)),
            dma((TP // 2,)),
            dma((TP // 2,)),
            dma((TP // 2,)),
            dma((TP // 2,)),
        ],
        compiler_params=pltpu.CompilerParams(
            collective_id=0, has_side_effects=True, vmem_limit_bytes=40 * 2**20
        ),
    )(
        *(
            pltpu.with_memory_space_constraint(operand, pltpu.HBM)
            for operand in (
                moving.reshape(1, -1), destination.reshape(1, -1), round_pages.T, lengths,
                kv_cache, queries, fresh_kv, out_proj,
            )
        )
    )
    return attended, arrived


def solution(mesh):
    in_specs = (
        P("inst", None, "tp"),
        P("inst", None, "tp"),
        P("inst", None, "tp"),
        P("tp", None),
        P(),
        P(),
        P(),
        P(),
    )
    out_specs = (P("inst", None, "tp"), P("inst", None, "tp"))
    return jax.shard_map(local, mesh=mesh, in_specs=in_specs, out_specs=out_specs, check_vma=False)
```

time: 93.6 us -> 68.4 us (0.73)
  the two profiles are of different devices: /device:TPU:1 before, /device:TPU:4 now
where the time goes in v2:
time: 68.4 us; the launch traced here: 68.3 us
  Pallas kernels  65.1 us (95%)
  local copies, waits for them, and re-layouts  2.66 us (4%)
    pallas_call x1, Pallas kernels, local(): pl.pallas_call(kernel, out_shape=(pltpu.VMEM((slots, STEPS, COLS), bf16),...  65.1 us
    unnamed x2, local copies, waits for them, and re-layouts  2.66 us

profile of v2, /device:TPU:4, one launch (start us, length us, event | category | flops | bytes accessed | tf_op | source)
XLA Modules:
  0.0 68.3 jit_solution(12559751597854389841)
XLA Ops:
  0.6 65.1 %shard_map.95 = (bf16[12,6,512]{2,1,0:T(8,128)(2,1)S(1)}, bf16[4,2048,256]{2,1,0:T(8,128)(2,1)S(1)}) custom-call(s32[1,128]{1,0:T(1,128)} %bitcast.4, s32[1,128]{1,0:T(1,128)} %bitcast.5, s32[3,128]{1,0:T(4,128)} %bitcast.3, s32[256]{0:T(256)} %lengths_hbm.1, bf16[8,2048,256]{2,1,0:T(8,128)(2,1)} %kv_hbm.1, bf16[12,6,1024]{2,1,0:T(8,128)(2,1)} %q_hbm.1, ...), custom_call_target="tpu_custom_call" | custom-call | tf_op jit(solution)/shard_map/pallas_call | solution.py:448
  65.7 0.6 copy.12
  66.3 2.0 %copy.13 = bf16[4,2048,256]{2,1,0:T(8,128)(2,1)} copy(bf16[4,2048,256]{2,1,0:T(8,128)(2,1)S(1)} %get-tuple-element.3) | data formatting | bytes 8388608

commit v3 on v2

--- a/solution.py
+++ b/solution.py
@@ -30,27 +30,32 @@
 SCALE = HEAD_DIM**-0.5
 
 RELAYS = (
-    (0, 15, 0, 0, 0, 12),
+    (0, 7, 11, 0, 0, 4),
+    (0, 15, 0, 0, 0, 4),
+    (0, 15, 3, 0, 4, 8),
     (1, 0, 3, 0, 0, 4),
-    (1, 2, 6, 0, 0, 8),
+    (1, 2, 5, 0, 0, 4),
+    (1, 2, 7, 0, 4, 8),
     (1, 4, 7, 0, 0, 4),
-    (1, 6, 10, 0, 0, 12),
+    (1, 6, 9, 0, 0, 4),
     (1, 8, 11, 0, 0, 4),
-    (1, 10, 9, 0, 0, 8),
-    (1, 10, 14, 0, 8, 16),
+    (1, 10, 14, 0, 0, 4),
+    (1, 10, 15, 0, 4, 8),
     (1, 12, 15, 0, 0, 4),
-    (1, 14, 1, 0, 0, 12),
-    (1, 15, 2, 0, 0, 12),
+    (1, 14, 1, 0, 0, 8),
+    (1, 15, 1, 0, 0, 4),
+    (1, 15, 2, 0, 4, 12),
     (2, 0, 12, 0, 0, 12),
-    (2, 1, 13, 0, 0, 4),
+    (2, 1, 13, 0, 0, 8),
     (2, 8, 4, 0, 0, 12),
     (2, 9, 5, 0, 0, 4),
-    (2, 10, 6, 0, 0, 4),
-    (2, 11, 3, 0, 0, 4),
+    (2, 10, 2, 0, 0, 4),
+    (2, 11, 7, 0, 0, 4),
     (2, 12, 8, 0, 0, 4),
     (2, 13, 5, 0, 0, 4),
-    (2, 14, 6, 0, 0, 8),
-    (2, 15, 7, 0, 0, 12),
+    (2, 14, 6, 0, 0, 12),
+    (2, 15, 3, 0, 0, 8),
+    (2, 15, 7, 0, 8, 16),
 )
 
 
@@ -436,6 +441,15 @@
 
     for lane in range(LANES):
         bulk_copy(lane, 0, CACHE).wait_recv()
+
+
+def write_out(att_ref, cache_ref, att_out, cache_out, sem):
+    copies = [pltpu.make_async_copy(cache_ref.at[lane], cache_out.at[lane], sem.at[lane]) for lane in range(LANES)]
+    copies.append(pltpu.make_async_copy(att_ref, att_out, sem.at[LANES]))
+    for copy in copies:
+        copy.start()
+    for copy in copies:
+        copy.wait()
 
 
 def local(kv_cache, queries, fresh_kv, out_proj, moving, destination, round_pages, lengths):
@@ -505,7 +519,17 @@
             )
         )
     )
-    return attended, arrived
+    return pl.pallas_call(
+        write_out,
+        out_shape=(
+            pltpu.HBM((slots, STEPS, COLS), bf16),
+            pltpu.HBM((LANES, CACHE, row_width), bf16),
+        ),
+        in_specs=[vmem, vmem],
+        out_specs=(hbm, hbm),
+        scratch_shapes=[dma((LANES + 1,))],
+        compiler_params=pltpu.CompilerParams(vmem_limit_bytes=16 * 2**20),
+    )(pltpu.with_memory_space_constraint(attended, pltpu.VMEM), pltpu.with_memory_space_constraint(arrived, pltpu.VMEM))
 
 
 def solution(mesh):

time: 68.4 us -> 65.9 us (0.963)
  the two profiles are of different devices: /device:TPU:4 before, /device:TPU:1 now
where the time goes in v3:
time: 65.9 us; the launch traced here: 65.5 us
  Pallas kernels  64.8 us (98%)
    pallas_call x1, Pallas kernels, local(): pl.pallas_call(kernel, out_shape=(pltpu.VMEM((slots, STEPS, COLS), bf16),...  62.8 us
    pallas_call x1, Pallas kernels, local(): pl.pallas_call(write_out, out_shape=(pltpu.HBM((slots, STEPS, COLS), bf16...  2.07 us

profile of v3, /device:TPU:1, one launch (start us, length us, event | category | flops | bytes accessed | tf_op | source)
XLA Modules:
  0.0 65.5 jit_solution(9918236313770098212)
XLA Ops:
  0.6 62.8 %shard_map.95 = (bf16[12,6,512]{2,1,0:T(8,128)(2,1)S(1)}, bf16[4,2048,256]{2,1,0:T(8,128)(2,1)S(1)}) custom-call(s32[1,128]{1,0:T(1,128)} %bitcast.4, s32[1,128]{1,0:T(1,128)} %bitcast.5, s32[3,128]{1,0:T(4,128)} %bitcast.3, s32[256]{0:T(256)} %lengths_hbm.1, bf16[8,2048,256]{2,1,0:T(8,128)(2,1)} %kv_hbm.1, bf16[12,6,1024]{2,1,0:T(8,128)(2,1)} %q_hbm.1, ...), custom_call_target="tpu_custom_call" | custom-call | tf_op jit(solution)/shard_map/pallas_call | solution.py:462
  63.4 2.1 %shard_map.96 = (bf16[12,6,512]{2,1,0:T(8,128)(2,1)}, bf16[4,2048,256]{2,1,0:T(8,128)(2,1)}) custom-call(bf16[12,6,512]{2,1,0:T(8,128)(2,1)S(1)} %get-tuple-element.4.att_ref, bf16[4,2048,256]{2,1,0:T(8,128)(2,1)S(1)} %get-tuple-element.5.cache_ref), custom_call_target="tpu_custom_call" | custom-call | tf_op jit(solution)/shard_map/pallas_call | solution.py:522

commit v4 on v3

--- a/solution.py
+++ b/solution.py
@@ -23,7 +23,9 @@
 CHUNKS = CACHE // CHUNK
 TAIL = 256
 DEPTH = 3
-LAG = 5
+FREE = 11
+DEPTH_LATE = 6
+LAG = 6
 HOPS = (2, 1, 3, 0)
 PACE = ((3, 3), (3, 4), (4, 4), (4, 5), (5, 6), (6, 6), (6, 7), (7, 8), (8, 8), (8, 8), (8, 9), (9, 9), (9, 9), (9, 10), (10, 10), (10, 10), (10, 11), (11, 16))
 MASKED = -1e30
@@ -297,12 +299,15 @@
                         landed(slot).wait_recv()
                         second_leg(slot, *pieces[slot]).start()
 
+    def gone(step):
+        return max(0, min(step, FREE) - DEPTH + 1, step - DEPTH_LATE + 1)
+
     def migrate(first, last):
         for step in range(first, last):
             if step < CHUNKS:
                 for lane in range(LANES):
-                    if step >= DEPTH:
-                        bulk_copy(lane, (step - DEPTH) * CHUNK, CHUNK).wait_send()
+                    for chunk in range(gone(step - 1), gone(step)):
+                        bulk_copy(lane, chunk * CHUNK, CHUNK).wait_send()
                     start_lane(lane, step)
             if step >= LAG:
                 forward(step - LAG)
@@ -425,7 +430,7 @@
     for lane in range(LANES):
         ask_copy(lane).wait_send()
         head_copy(lane).wait_send()
-        for chunk in range(CHUNKS - DEPTH, CHUNKS):
+        for chunk in range(gone(CHUNKS - 1), CHUNKS):
             bulk_copy(lane, chunk * CHUNK, CHUNK).wait_send()
     for hop in HOPS:
         pair_copy(hop).wait_send()

time: 65.9 us -> 65.2 us (0.989)
  Pallas kernels: 64.8 us -> 63.9 us
    pallas_call x1, Pallas kernels: 62.8 us -> 61.8 us  [local(): pl.pallas_call(kernel, out_shape=(pltpu.VMEM((slots, STEPS, COLS), bf16),...]
where the time goes in v4:
time: 65.2 us; the launch traced here: 64.6 us
  Pallas kernels  63.9 us (98%)
    pallas_call x1, Pallas kernels, local(): pl.pallas_call(kernel, out_shape=(pltpu.VMEM((slots, STEPS, COLS), bf16),...  61.8 us
    pallas_call x1, Pallas kernels, local(): pl.pallas_call(write_out, out_shape=(pltpu.HBM((slots, STEPS, COLS), bf16...  2.07 us

profile of v4, /device:TPU:1, one launch (start us, length us, event | category | flops | bytes accessed | tf_op | source)
XLA Modules:
  0.0 64.6 jit_solution(3417353484973192925)
XLA Ops:
  0.6 61.8 %shard_map.95 = (bf16[12,6,512]{2,1,0:T(8,128)(2,1)S(1)}, bf16[4,2048,256]{2,1,0:T(8,128)(2,1)S(1)}) custom-call(s32[1,128]{1,0:T(1,128)} %bitcast.4, s32[1,128]{1,0:T(1,128)} %bitcast.5, s32[3,128]{1,0:T(4,128)} %bitcast.3, s32[256]{0:T(256)} %lengths_hbm.1, bf16[8,2048,256]{2,1,0:T(8,128)(2,1)} %kv_hbm.1, bf16[12,6,1024]{2,1,0:T(8,128)(2,1)} %q_hbm.1, ...), custom_call_target="tpu_custom_call" | custom-call | tf_op jit(solution)/shard_map/pallas_call | solution.py:467
  62.5 2.1 %shard_map.96 = (bf16[12,6,512]{2,1,0:T(8,128)(2,1)}, bf16[4,2048,256]{2,1,0:T(8,128)(2,1)}) custom-call(bf16[12,6,512]{2,1,0:T(8,128)(2,1)S(1)} %get-tuple-element.4.att_ref, bf16[4,2048,256]{2,1,0:T(8,128)(2,1)S(1)} %get-tuple-element.5.cache_ref), custom_call_target="tpu_custom_call" | custom-call | tf_op jit(solution)/shard_map/pallas_call | solution.py:527
